TPU v7x, 32 devices: a whole 2x2x4 slice. The times are simulated.
32 devices in a mesh: src: 8 (over z, core), rcv: 2 (over y), int: 2 (over x).
Axes of the slice: x: 2, y: 2, z: 4, core: 2. Of those that a mesh axis runs over, the one named last changes fastest.
Arguments:
- traces: float32 [2, 1, 4096, 4096], P(None, None, 'src', 'rcv'), may hold values from -6 to 6
- missing: int32 [32, 32], P('src', 'rcv'), may hold values from 0 to 1, as said below
- aperture: int32 [32, 24], P('src'), may hold values from 0 to 32, as said below
- wavelet: float32 [2, 1], replicated, may hold values from -0.06 to 0.06
Outputs:
- primaries: float32 [2, 1, 4096, 4096], P(None, None, 'src', ('rcv', 'int'))
Inputs may be any that keep to these rules, and one draw needn't show every extreme that they name: `missing`: A tile is marked only where its receiver block lies above its source block, so the mirrored tile is always recorded; some tile is marked. `aperture`: in each row the listed blocks come first and are distinct; the remaining entries are the padding value 32. Each row lists 24 // 2 to 24 blocks; some row lists exactly 24 and some row exactly 12.
All inputs are finite; a program needn't handle non-finite values.
Results may differ from a plain program's by a relative error of at most 0.00005.
Values sent between devices are 32-bit elements; how exact they have to be, the bound alone decides.
A program may use at most 128 MiB of HBM per device.

v0:
```python
import jax
import jax.numpy as jnp
from jax import lax
from jax.sharding import PartitionSpec as P

TILE = 128


def complex_prod(left_side, right_side):
    return jnp.einsum("fik,fkj->fij", left_side, right_side, precision=lax.Precision.HIGHEST)


def per_device(traces, missing, aperture, wavelet):
    half_count = lax.axis_size("int")
    my_half = lax.axis_index("int")
    rcv_count = lax.axis_size("rcv")
    comp_count, freq_count, local_rows, local_cols = traces.shape
    regrouped = lax.all_to_all(traces, "rcv", split_axis=2, concat_axis=3, tiled=True)
    sectioned = regrouped.reshape(
        comp_count, freq_count, 1, local_rows // rcv_count, local_cols * rcv_count
    )
    arrived = lax.all_to_all(
        lax.all_to_all(sectioned, "src", split_axis=4, concat_axis=2, tiled=True),
        "rcv",
        split_axis=2,
        concat_axis=3,
        tiled=True,
    )
    mirrored = jnp.swapaxes(arrived.reshape(comp_count, freq_count, local_cols, local_rows), 2, 3)
    row_tiles = local_rows // TILE
    col_tiles = local_cols // TILE
    tile_mask = jnp.broadcast_to(
        missing[:, None, :, None] > 0, (row_tiles, TILE, col_tiles, TILE)
    ).reshape(local_rows, local_cols)
    filled = jnp.where(tile_mask[None, None], mirrored, traces)
    half_tile = TILE // half_count
    left_half = filled.reshape(comp_count, freq_count, local_rows, col_tiles, half_count, half_tile)
    left_half = lax.dynamic_index_in_dim(left_half, my_half, 4, keepdims=False)
    left_half = left_half.reshape(comp_count, freq_count, local_rows, col_tiles * half_tile)
    right_half = filled.reshape(
        comp_count, freq_count, row_tiles, half_count, half_tile, local_cols
    )
    right_half = lax.dynamic_index_in_dim(right_half, my_half, 3, keepdims=False)
    right_half = right_half.reshape(comp_count, freq_count, row_tiles * half_tile, local_cols)
    gathered = lax.all_gather(left_half, "rcv", axis=3, tiled=True)
    block_count = gathered.shape[3] // half_tile
    chosen = (
        (aperture[:, :, None] == jnp.arange(block_count, dtype=jnp.int32)[None, None, :])
        .astype(jnp.float32)
        .sum(axis=1)
    )
    weighted = gathered.reshape(comp_count, freq_count, row_tiles, TILE, block_count, half_tile)
    weighted = (weighted * chosen[None, None, :, None, :, None]).reshape(
        comp_count, freq_count, local_rows, block_count * half_tile
    )
    slab_piece = lax.all_gather(right_half, "src", axis=2, tiled=True)
    real_part = complex_prod(weighted[0], slab_piece[0]) - complex_prod(weighted[1], slab_piece[1])
    imag_part = complex_prod(weighted[0], slab_piece[1]) + complex_prod(weighted[1], slab_piece[0])
    partial_sum = jnp.stack([real_part, imag_part])
    out_cols = local_cols // half_count
    my_share = lax.psum_scatter(partial_sum, "int", scatter_dimension=3, tiled=True)
    kept_data = filled.reshape(comp_count, freq_count, local_rows, half_count, out_cols)
    kept_data = lax.dynamic_index_in_dim(kept_data, my_half, 3, keepdims=False)
    w_real = wavelet[0][:, None, None]
    w_imag = wavelet[1][:, None, None]
    out_real = kept_data[0] - (w_real * my_share[0] - w_imag * my_share[1])
    out_imag = kept_data[1] - (w_real * my_share[1] + w_imag * my_share[0])
    return jnp.stack([out_real, out_imag])


def solution(mesh):
    placed = (P(None, None, "src", "rcv"), P("src", "rcv"), P("src", None), P())
    return jax.shard_map(
        per_device,
        mesh=mesh,
        in_specs=placed,
        out_specs=P(None, None, "src", ("rcv", "int")),
        check_vma=False,
    )
```

profile of v0, /device:TPU:29, one launch (start us, length us, event | category | flops | bytes accessed | tf_op | source)
XLA Modules:
  0.0 1105.0 jit_solution(1004001187149340830)
XLA Ops:
  6.5 14.4 %copy.29 = f32[2,1,512,2048]{3,0,1,2:T(2,128)S(1)} copy(f32[2,1,512,2048]{3,2,1,0:T(8,128)} %param.4) | data formatting | bytes 16777216 | tf_op args[0]
  20.9 93.8 %all_to_all.48 = f32[2,1,512,2048]{3,0,1,2:T(2,128)S(1)} all-to-all(f32[2,1,512,2048]{3,0,1,2:T(2,128)S(1)} %copy.29), channel_id=1, replica_groups=mesh['src'=8,'rcv'=2,'int'=2] {'rcv'}, dimensions={2} | all-to-all | bytes 16777216 | tf_op jit(solution)/shard_map/all_to_all | solution.py:18
  114.8 8.1 copy.30
  122.9 8.7 copy.31
  131.6 14.4 %copy.32 = f32[2,1,1,256,4096]{3,0,2,1,4:T(2,128)S(1)} copy(f32[2,1,1,256,4096]{3,4,0,2,1:T(8,128)} %bitcast.79) | data formatting | bytes 16777216 | tf_op jit(solution)/shard_map/reshape | solution.py:19
  146.0 187.1 %all_to_all.49 = f32[2,1,1,256,4096]{3,0,2,1,4:T(2,128)} all-to-all(f32[2,1,1,256,4096]{3,0,2,1,4:T(2,128)S(1)} %copy.32), channel_id=1, replica_groups=mesh['src'=8,'rcv'=2,'int'=2] {'src'}, dimensions={4} | all-to-all | bytes 16777216 | tf_op jit(solution)/shard_map/all_to_all | solution.py:23
  333.1 13.2 %copy.33 = f32[2,1,1,256,8,512]{5,3,0,4,2,1:T(8,128)} copy(f32[2,1,1,256,8,512]{3,0,5,4,2,1:T(2,128)} %bitcast.80) | data formatting | bytes 16777216 | tf_op jit(solution)/shard_map/all_to_all | solution.py:23
  346.2 8.4 all-to-all-start.2
  354.6 0.0 copy-start.2
  354.6 0.2 all-gather.3.cloned.1.call-start
  354.9 8.7 copy.36
  363.5 0.0 copy-done.2
  363.6 0.1 copy.28
  363.7 0.6 broadcast_in_dim.12
  364.3 0.5 copy.67
  364.8 80.7 %all-to-all-done.2 = f32[2,1,8,256,512]{4,3,0,1,2:T(8,128)} async-done(((f32[2,1,8,256,512]{4,3,0,1,2:T(8,128)}), f32[2,1,8,256,512]{4,3,0,1,2:T(8,128)}, u32[]{:S(2)}, u32[]{:S(2)}) %all-to-all-start.2) | async-done | bytes 8388640 | tf_op jit(solution)/shard_map/all_to_all | solution.py:22
  445.5 4.4 copy.34
  449.9 4.3 copy.35
  454.2 11.2 %bitcast_select_fusion = f32[2,1,512,2048]{2,3,0,1:T(8,128)} fusion(f32[2,1,512,2048]{2,3,0,1:T(8,128)} %copy.36, f32[2,1,4,2,256,512]{5,4,3,2,0,1:T(8,128)} %copy.35, pred[512,2048]{0,1:T(8,128)(4,1)S(1)} %bitcast.85), kind=kLoop, calls=%fused_computation.7 | loop fusion | flops 2097152 | bytes 26214400 | tf_op jit(solution)/shard_map/jit(_where)/select_n | solution.py:35
  465.4 5.0 constant_dynamic-slice_fusion.2
  470.4 0.0 all-gather.3.cloned.1.call-update
  470.4 0.0 all-gather.5.cloned.1.call-start
  470.4 8.8 copy.39
  479.2 5.5 constant_dynamic-slice_fusion.1
  484.7 0.0 copy-start.3
  484.7 0.0 all-gather.5.cloned.1.call-update
  484.7 0.3 reduce-scatter.2.cloned.1.call-start
  485.0 0.4 copy-done.3
  485.3 0.1 convert_reduce_fusion
  485.4 0.1 copy.38
  485.5 89.6 %all-gather.3.cloned.1.call-done = f32[2,1,512,2048]{2,3,0,1:T(8,128)} async-done(((f32[2,1,512,1024]{2,3,0,1:T(8,128)}), f32[2,1,512,2048]{2,3,0,1:T(8,128)}) %all-gather.3.cloned.1.call-update) | async-done | bytes 8388624 | tf_op jit(solution)/shard_map/all_gather | solution.py:45
  575.1 9.9 reshape.123
  585.1 12.6 %broadcast_multiply_fusion = f32[2,1,4,128,32,64]{3,2,1,5,4,0:T(4,128)} fusion(f32[2,1,4,128,32,64]{3,2,1,5,4,0:T(4,128)} %reshape.123, f32[4,32]{0,1:T(8,128)S(1)} %copy.38), kind=kLoop, calls=%fused_computation.15 | loop fusion | flops 2097152 | bytes 16777728 | tf_op jit(solution)/shard_map/mul | solution.py:53
  597.7 7.9 fusion.16
  605.6 258.3 %all-gather.5.cloned.1.call-done = f32[2,1,2048,2048]{3,2,0,1:T(8,128)} async-done(((f32[2,1,256,2048]{3,2,0,1:T(8,128)}), f32[2,1,2048,2048]{3,2,0,1:T(8,128)}) %all-gather.5.cloned.1.call-update) | async-done | bytes 33554448 | tf_op jit(solution)/shard_map/all_gather | solution.py:56
  863.9 0.0 copy-start.1
  863.9 33.9 %fusion = f32[512,2048]{1,0:T(8,128)S(1)} fusion(f32[2,1,2048,2048]{3,2,0,1:T(8,128)} %all-gather.5.cloned.1.call-done, f32[256,8,4,128]{3,2,1,0:T(4,128)} %bitcast.87), kind=kOutput, calls=%fused_computation.2 | convolution fusion | flops 25769803776 | bytes 25165824 | tf_op jit(solution)/shard_map/fik,fkj->fij/dot_general | solution.py:10
  897.8 0.0 copy-done.1
  897.8 29.9 %fusion.1 = f32[512,2048]{1,0:T(8,128)S(1)} fusion(f32[2,1,2048,2048]{3,2,0,1:T(8,128)} %all-gather.5.cloned.1.call-done, f32[256,8,4,128]{3,2,1,0:T(4,128)S(1)} %bitcast.89), kind=kOutput, calls=%fused_computation.3 | convolution fusion | flops 25769803776 | bytes 25165824 | tf_op jit(solution)/shard_map/fik,fkj->fij/dot_general | solution.py:10
  927.7 0.0 copy-start
  927.7 29.8 %add_bitcast_fusion = f32[1,1,512,2048]{3,2,1,0:T(8,128)S(1)} fusion(f32[512,2048]{1,0:T(8,128)S(1)} %fusion, f32[2,1,2048,2048]{3,2,0,1:T(8,128)} %all-gather.5.cloned.1.call-done, f32[256,8,4,128]{3,2,1,0:T(4,128)S(1)} %bitcast.90), kind=kOutput, calls=%fused_computation.13 | convolution fusion | flops 25770852352 | bytes 29360128 | tf_op jit(solution)/shard_map/fik,fkj->fij/dot_general | solution.py:10
  957.5 0.0 copy-done
  957.5 29.7 %subtract_bitcast_fusion = f32[1,1,512,2048]{3,2,1,0:T(8,128)S(1)} fusion(f32[512,2048]{1,0:T(8,128)S(1)} %fusion.1, f32[2,1,2048,2048]{3,2,0,1:T(8,128)} %all-gather.5.cloned.1.call-done, f32[256,8,4,128]{3,2,1,0:T(4,128)S(1)} %bitcast.88), kind=kOutput, calls=%fused_computation.14 | convolution fusion | flops 25770852352 | bytes 29360128 | tf_op jit(solution)/shard_map/fik,fkj->fij/dot_general | solution.py:10
  987.2 3.8 pad_maximum_fusion
  991.0 0.0 copy-start.4
  991.0 0.0 reduce-scatter.2.cloned.1.call-update
  991.0 0.6 copy-done.4
  991.6 0.6 fusion.17
  992.2 4.6 constant_dynamic-slice_fusion
  996.8 1.9 copy.41
  998.7 3.0 copy.42
  1001.7 89.3 %reduce-scatter.2.cloned.1.call-done = f32[2,1,512,1024]{3,2,1,0:T(8,128)} async-done(((f32[2,1,512,2048]{3,2,1,0:T(8,128)}), f32[2,1,512,1024]{3,2,1,0:T(8,128)}) %reduce-scatter.2.cloned.1.call-update) | async-done | bytes 4194320 | tf_op jit(solution)/shard_map/reduce_scatter | solution.py:61
  1091.0 7.3 bitcast_subtract_fusion.1
  (2 shorter events, 0.0 us)
Async XLA Ops:
  346.2 99.3 %all-to-all-start.2 = ((f32[2,1,8,256,512]{4,3,0,1,2:T(8,128)}), f32[2,1,8,256,512]{4,3,0,1,2:T(8,128)}, u32[]{:S(2)}, u32[]{:S(2)}) async-start(f32[2,1,8,256,512]{4,3,0,1,2:T(8,128)} %bitcast.77), calls=%async_computation.2 | async-start | bytes 16777216 | tf_op jit(solution)/shard_map/all_to_all | solution.py:22
  354.6 8.9 copy-start.2
  354.6 220.5 %all-gather.3.cloned.1.call-start = ((), (), s32[]{:S(2)}) async-start(), calls=%async_computation.4 | async-start | bytes 12582912 | tf_op jit(solution)/shard_map/all_gather | solution.py:45
  470.4 393.5 %all-gather.5.cloned.1.call-start = ((), (), s32[]{:S(2)}) async-start(), calls=%async_computation.5 | async-start | bytes 37748736 | tf_op jit(solution)/shard_map/all_gather | solution.py:56
  484.7 0.7 copy-start.3
  484.7 606.3 %reduce-scatter.2.cloned.1.call-start = ((), (), s32[]{:S(2)}) async-start(), calls=%async_computation.6 | async-start | bytes 12582912 | tf_op jit(solution)/shard_map/reduce_scatter | solution.py:61
  863.9 33.9 %copy-start.1 = (f32[1,1,4,128,32,64]{3,2,1,5,4,0:T(4,128)S(1)}, f32[1,1,4,128,32,64]{3,2,1,5,4,0:T(4,128)}, u32[]{:S(2)}) copy-start(f32[1,1,4,128,32,64]{3,2,1,5,4,0:T(4,128)} %get-tuple-element.7) | copy-start | bytes 12582916
  927.7 29.8 %copy-start = (f32[1,1,4,128,32,64]{3,2,1,5,4,0:T(4,128)S(1)}, f32[1,1,4,128,32,64]{3,2,1,5,4,0:T(4,128)}, u32[]{:S(2)}) copy-start(f32[1,1,4,128,32,64]{3,2,1,5,4,0:T(4,128)} %get-tuple-element.8) | copy-start | bytes 12582916
  991.0 0.7 copy-start.4
Sparse Core Ops, SparseCore 0:
  470.5 104.5 all-gather.2
  576.7 287.1 all-gather.4
  991.1 99.8 reduce-scatter.1
where the time goes:
time: 1120 us; the launch traced here: 1110 us
  waiting for transfers between devices  518 us (46%)
  blocking collectives  281 us (25%)
  local copies, waits for them, and re-layouts  125 us (11%)
  matrix products  123 us (11%)
  other arithmetic  35 us (3%)
  between operations  13.5 us (1%)
    all_gather x1, waiting for transfers between devices, per_device(): slab_piece = lax.all_gather(right_half, 'src', axis=2, tiled=True)  258 us
    all_to_all x1, blocking collectives, per_device(): lax.all_to_all(sectioned, 'src', split_axis=4, concat_axis=2, tiled=True)  187 us
    dot_general x4, matrix products, complex_prod(): jnp.einsum('fik,fkj->fij', left_side, right_side, precision=lax.Precision...  123 us
    all_to_all x1, blocking collectives, per_device(): lax.all_to_all(traces, 'rcv', split_axis=2, concat_axis=3, tiled=True)  93.8 us
    all_gather x1, waiting for transfers between devices, per_device(): gathered = lax.all_gather(left_half, 'rcv', axis=3, tiled=True)  89.6 us
    reduce_scatter x1, waiting for transfers between devices, per_device(): lax.psum_scatter(partial_sum, 'int', scatter_dimension=3, tiled=True)  89.3 us
    all_to_all x1, waiting for transfers between devices, per_device(): lax.all_to_all(lax.all_to_all(sectioned, 'src', split_axis=4, concat_axis...  80.7 us
    unnamed x15, local copies, waits for them, and re-layouts  29.5 us
  transfers between devices with their start and end apart: 4, of which 4 were waited for; matrix products, arithmetic and copies ran while one was open for 6% of the time, Pallas kernels for 0%

commit v1 on v0

v1 whole, which is shorter than its diff:
```python
import jax
import jax.numpy as jnp
from jax import lax
from jax.sharding import PartitionSpec as P

TILE = 128
EVERY = ("src", "rcv", "int")


def product(left_side, right_side):
    return jnp.dot(left_side, right_side, precision=lax.Precision.HIGH)


def mirror_pairs(src_count, rcv_count, int_count, half):
    col_count = rcv_count * int_count
    pairs = []
    for s in range(src_count):
        for q in range(col_count):
            if s >= 2 * q + half:
                pairs.append((s * col_count + q, (2 * q + half) * col_count + s // 2))
    return pairs


def per_device(traces, missing, aperture, wavelet):
    src_count, rcv_count, int_count = (lax.axis_size(a) for a in EVERY)
    col_count = rcv_count * int_count
    assert src_count == 2 * col_count
    rows, wide = traces.shape[2], traces.shape[3]
    cols = wide // int_count
    my_int = lax.axis_index("int")
    s = lax.axis_index("src")
    own = lax.dynamic_slice_in_dim(traces[:, 0], my_int * cols, cols, axis=2)
    arrived = []
    for half in (0, 1):
        part = own[:, :, half * rows : (half + 1) * rows]
        for sender in (0, 1):
            pairs = [
                (a, b)
                for a, b in mirror_pairs(src_count, rcv_count, int_count, half)
                if (a // col_count) % 2 == sender
            ]
            arrived.append(lax.ppermute(part, EVERY, pairs))
    odd = (s % 2) == 1
    first = jnp.where(odd, arrived[2], arrived[0])
    second = jnp.where(odd, arrived[3], arrived[1])
    mirrored = jnp.concatenate([jnp.swapaxes(first, 1, 2), jnp.swapaxes(second, 1, 2)], axis=2)
    row_tiles, col_tiles = rows // TILE, cols // TILE
    my_missing = lax.dynamic_slice_in_dim(missing, my_int * col_tiles, col_tiles, axis=1)
    mask = jnp.repeat(jnp.repeat(my_missing > 0, TILE, axis=0), TILE, axis=1)
    filled = jnp.where(mask[None], mirrored, own)
    left = lax.all_gather(filled, ("rcv", "int"), axis=0)
    right = lax.all_gather(filled, "src", axis=1, tiled=True)
    blocks = col_count * col_tiles
    chosen = (
        (aperture[:, :, None] == jnp.arange(blocks, dtype=jnp.int32)[None, None, :])
        .astype(jnp.float32)
        .sum(axis=1)
    )
    scale = jnp.repeat(jnp.repeat(chosen, TILE, axis=0), TILE, axis=1)
    left = jnp.moveaxis(left, 0, 2).reshape(2, rows, col_count * cols) * scale[None]
    first_prod = product(left[0], right[0])
    second_prod = product(left[1], right[1])
    third_prod = product(left[0] + left[1], right[0] + right[1])
    real = first_prod - second_prod
    imag = third_prod - first_prod - second_prod
    w_real, w_imag = wavelet[0, 0], wavelet[1, 0]
    out_real = filled[0] - (w_real * real - w_imag * imag)
    out_imag = filled[1] - (w_real * imag + w_imag * real)
    return jnp.stack([out_real, out_imag])[:, None]


def solution(mesh):
    placed = (P(None, None, "src", "rcv"), P("src", "rcv"), P("src", None), P())
    return jax.shard_map(
        per_device,
        mesh=mesh,
        in_specs=placed,
        out_specs=P(None, None, "src", ("rcv", "int")),
        check_vma=False,
    )
```

time: 1120 us -> 841 us (0.75)
  blocking collectives: 281 us -> 0 us
  waiting for transfers between devices: 518 us -> 645 us
  local copies, waits for them, and re-layouts: 125 us -> 48.3 us
  matrix products: 123 us -> 80.6 us
    all_to_all x2 -> x0, blocking collectives: 281 us -> none  [the longest x1 187 us: per_device(): lax.all_to_all(sectioned, 'src', split_axis=4, concat_axis=2, tiled=True)]
    all_gather x2, waiting for transfers between devices: 348 us -> 575 us  [the longest x1 318 us: per_device(): left = lax.all_gather(filled, ('rcv', 'int'), axis=0)]
    reduce_scatter x1 -> x0, waiting for transfers between devices: 89.3 us -> none  [per_device(): lax.psum_scatter(partial_sum, 'int', scatter_dimension=3, tiled=True)]
    all_to_all x1 -> x0, waiting for transfers between devices: 80.7 us -> none  [per_device(): lax.all_to_all(lax.all_to_all(sectioned, 'src', split_axis=4, concat_axis...]
    ppermute x0 -> x4, waiting for transfers between devices: none -> 70.2 us  [per_device(): arrived.append(lax.ppermute(part, EVERY, pairs))]
    dot_general x4 -> x3, matrix products: 123 us -> 80.6 us  [product(): return jnp.dot(left_side, right_side, precision=lax.Precision.HIGH)]
    all_to_all x5 -> x0, local copies, waits for them, and re-layouts: 38.6 us -> none  [the longest x2 16.8 us: per_device(): lax.all_to_all(traces, 'rcv', split_axis=2, concat_axis=3, tiled=True)]
    unnamed x15 -> x11, local copies, waits for them, and re-layouts: 29.5 us -> 1.99 us
  transfers between devices with their start and end apart: 4 -> 6, of which waited for: 4 -> 4; matrix products, arithmetic and copies ran while one was open for 6% -> 7% of each run, Pallas kernels for 0% -> 0%
where the time goes in v1:
time: 841 us; the launch traced here: 835 us
  waiting for transfers between devices  645 us (77%)
  matrix products  80.6 us (10%)
  local copies, waits for them, and re-layouts  48.3 us (6%)
  other arithmetic  36.5 us (4%)
  between operations  13.5 us (2%)
  starting transfers between devices  10.5 us (1%)
    all_gather x1, waiting for transfers between devices, per_device(): left = lax.all_gather(filled, ('rcv', 'int'), axis=0)  318 us
    all_gather x1, waiting for transfers between devices, per_device(): right = lax.all_gather(filled, 'src', axis=1, tiled=True)  257 us
    dot_general x3, matrix products, product(): return jnp.dot(left_side, right_side, precision=lax.Precision.HIGH)  80.6 us
    ppermute x4, waiting for transfers between devices, per_device(): arrived.append(lax.ppermute(part, EVERY, pairs))  70.2 us
    all_gather x1, local copies, waits for them, and re-layouts, per_device(): left = lax.all_gather(filled, ('rcv', 'int'), axis=0)  17.2 us
  transfers between devices with their start and end apart: 6, of which 4 were waited for; matrix products, arithmetic and copies ran while one was open for 7% of the time, Pallas kernels for 0%

profile of v1, /device:TPU:29, one launch (start us, length us, event | category | flops | bytes accessed | tf_op | source)
XLA Modules:
  0.0 834.6 jit_solution(2583275355453824424)
XLA Ops:
  6.5 0.0 all-gather.3.cloned.1.call-start
  6.5 2.5 fusion.37
  9.0 2.6 fusion.31
  11.6 0.8 collective-permute-start
  12.4 2.0 collective-permute-start.1
  14.4 4.9 collective-permute-start.2
  19.3 2.6 collective-permute-start.3
  21.9 4.8 constant_dynamic-slice_fusion
  26.7 0.0 copy-start.2
  26.7 5.4 copy.22
  32.1 0.0 copy-done.2
  32.1 0.1 dynamic-slice_compare_fusion
  32.2 0.1 broadcast_bitcast_fusion
  32.2 0.0 collective-permute-done
  32.2 0.0 copy-start.1
  32.2 1.3 copy-done.1
  33.6 0.0 collective-permute-done.1
  33.6 2.1 fusion.27
  35.7 0.0 copy-start
  35.7 28.0 %collective-permute-done.2 = f32[2,512,512]{2,1,0:T(8,128)} collective-permute-done((f32[2,512,512]{2,1,0:T(8,128)}, f32[2,512,512]{2,1,0:T(8,128)}, u32[]{:S(2)}, u32[]{:S(2)}) %collective-permute-start.2) | collective-permute-done | bytes 2097184 | tf_op jit(solution)/shard_map/ppermute | solution.py:42
  63.7 42.1 %collective-permute-done.3 = f32[2,512,512]{2,1,0:T(8,128)} collective-permute-done((f32[2,512,512]{2,1,0:T(8,128)}, f32[2,512,512]{2,1,0:T(8,128)}, u32[]{:S(2)}, u32[]{:S(2)}) %collective-permute-start.3) | collective-permute-done | bytes 2097184 | tf_op jit(solution)/shard_map/ppermute | solution.py:42
  105.9 3.4 fusion.29
  109.3 0.1 broadcast_in_dim.30
  109.4 0.0 copy-done
  109.4 3.1 maximum_select_fusion
  112.6 5.4 copy.23
  118.0 0.0 all-gather.3.cloned.1.call-update
  118.0 0.2 all-gather.5.cloned.1.call-start
  118.3 0.9 copy.20
  119.2 4.0 pad_maximum_fusion
  123.3 5.4 copy.21
  128.7 6.9 broadcast_select_fusion
  135.6 0.0 copy-start.3
  135.6 0.0 copy-start.4
  135.6 0.0 all-gather.5.cloned.1.call-update
  135.6 0.7 copy-done.3
  136.3 0.1 convert_reduce_fusion
  136.4 0.1 copy.25
  136.5 0.1 broadcast_in_dim.34
  136.6 0.0 copy-done.4
  136.6 0.6 fusion.32
  137.2 318.1 %all-gather.3.cloned.1.call-done = f32[4,2,512,1024]{3,2,1,0:T(8,128)} async-done(((f32[1,2,512,1024]{3,2,1,0:T(8,128)}), f32[4,2,512,1024]{3,2,1,0:T(8,128)}) %all-gather.3.cloned.1.call-update) | async-done | bytes 16777232 | tf_op jit(solution)/shard_map/all_gather | solution.py:51
  455.2 17.2 %copy.24 = f32[4,2,512,1024]{2,3,0,1:T(8,128)} copy(f32[4,2,512,1024]{3,2,1,0:T(8,128)} %all-gather.3.cloned.1.call-done) | data formatting | bytes 33554432 | tf_op jit(solution)/shard_map/all_gather | solution.py:51
  472.5 1.1 broadcast_in_dim.35
  473.5 12.7 %bitcast_multiply_fusion = f32[2,512,4096]{1,2,0:T(8,128)} fusion(f32[4,2,512,1024]{2,3,0,1:T(8,128)} %copy.24, f32[512,4096]{0,1:T(8,128)S(1)} %bitcast.77), kind=kLoop, calls=%fused_computation | loop fusion | flops 4194304 | bytes 41943040 | tf_op jit(solution)/shard_map/mul | solution.py:60
  486.3 256.9 %all-gather.5.cloned.1.call-done = f32[2,4096,1024]{2,1,0:T(8,128)} async-done(((f32[2,512,1024]{2,1,0:T(8,128)}), f32[2,4096,1024]{2,1,0:T(8,128)}) %all-gather.5.cloned.1.call-update) | async-done | bytes 33554448 | tf_op jit(solution)/shard_map/all_gather | solution.py:52
  743.1 19.7 %fusion.2 = f32[512,1024]{1,0:T(8,128)} fusion(f32[2,4096,1024]{2,1,0:T(8,128)} %all-gather.5.cloned.1.call-done, f32[2,512,4096]{1,2,0:T(8,128)} %bitcast_multiply_fusion), kind=kOutput, calls=%fused_computation.3 | convolution fusion | flops 12884901888 | bytes 27262976 | tf_op jit(solution)/shard_map/dot_general | solution.py:11
  762.8 19.8 %fusion.4 = f32[512,1024]{1,0:T(8,128)} fusion(f32[2,4096,1024]{2,1,0:T(8,128)} %all-gather.5.cloned.1.call-done, f32[2,512,4096]{1,2,0:T(8,128)} %bitcast_multiply_fusion), kind=kOutput, calls=%fused_computation.5 | convolution fusion | flops 12884901888 | bytes 27262976 | tf_op jit(solution)/shard_map/dot_general | solution.py:11
  782.6 41.1 %fusion.22 = (f32[1,512,1024]{2,1,0:T(8,128)S(1)}, f32[1,512,1024]{2,1,0:T(8,128)}) fusion(f32[2,512,1024]{2,1,0:T(8,128)} %broadcast_select_fusion, f32[]{:T(128)} %bitcast.17, f32[]{:T(128)} %bitcast.6, f32[512,1024]{1,0:T(8,128)} %fusion.4, f32[512,1024]{1,0:T(8,128)} %fusion.2, f32[2,4096,1024]{2,1,0:T(8,128)} %all-gather.5.cloned.1.call-done, ...), kind=kOutput, calls=%fused_computation.28 | convolution fusion | flops 12896960512 | bytes 62914568 | tf_op jit(solution)/shard_map/dot_general | solution.py:11
  823.7 4.0 maximum_bitcast_fusion
  (1 shorter events, 0.0 us)
Async XLA Ops:
  6.5 448.7 %all-gather.3.cloned.1.call-start = ((), (), s32[]{:S(2)}) async-start(), calls=%async_computation | async-start | bytes 20971520 | tf_op jit(solution)/shard_map/all_gather | solution.py:51
  11.6 20.6 %collective-permute-start = (f32[2,512,512]{2,1,0:T(8,128)}, f32[2,512,512]{2,1,0:T(8,128)S(1)}, u32[]{:S(2)}, u32[]{:S(2)}) collective-permute-start(f32[2,512,512]{2,1,0:T(8,128)} %get-tuple-element.12), channel_id=1, source_target_pairs={{8,5},{16,6},{17,14},{24,7},{25,15},{26,23}} | collective-permute-start | bytes 6291464 | tf_op jit(solution)/shard_map/ppermute | solution.py:42
  12.4 21.2 %collective-permute-start.1 = (f32[2,512,512]{2,1,0:T(8,128)}, f32[2,512,512]{2,1,0:T(8,128)}, u32[]{:S(2)}, u32[]{:S(2)}) collective-permute-start(f32[2,512,512]{2,1,0:T(8,128)} %get-tuple-element.11), channel_id=1, source_target_pairs={{0,0},{8,1},{9,9},{16,2},{17,10},{18,18},{24,3},{25,11},{26,19},{2... | collective-permute-start | bytes 6291464 | tf_op jit(solution)/shard_map/ppermute | solution.py:42
  14.4 49.3 %collective-permute-start.2 = (f32[2,512,512]{2,1,0:T(8,128)}, f32[2,512,512]{2,1,0:T(8,128)}, u32[]{:S(2)}, u32[]{:S(2)}) collective-permute-start(f32[2,512,512]{2,1,0:T(8,128)} %get-tuple-element.12), channel_id=1, source_target_pairs={{4,4},{12,5},{13,13},{20,6},{21,14},{22,22},{28,7},{29,15},{30,23}... | collective-permute-start | bytes 6291464 | tf_op jit(solution)/shard_map/ppermute | solution.py:42
  19.3 86.6 %collective-permute-start.3 = (f32[2,512,512]{2,1,0:T(8,128)}, f32[2,512,512]{2,1,0:T(8,128)}, u32[]{:S(2)}, u32[]{:S(2)}) collective-permute-start(f32[2,512,512]{2,1,0:T(8,128)} %get-tuple-element.11), channel_id=1, source_target_pairs={{4,0},{12,1},{13,9},{20,2},{21,10},{22,18},{28,3},{29,11},{30,19},... | collective-permute-start | bytes 6291464 | tf_op jit(solution)/shard_map/ppermute | solution.py:42
  26.7 5.4 copy-start.2
  32.2 1.3 copy-start.1
  35.7 73.8 %copy-start = (f32[2,1,512,1024]{2,3,0,1:T(8,128)S(1)}, f32[2,1,512,1024]{2,3,0,1:T(8,128)}, u32[]{:S(2)}) copy-start(f32[2,1,512,1024]{2,3,0,1:T(8,128)} %copy.22) | copy-start | bytes 12582916
  118.0 625.1 %all-gather.5.cloned.1.call-start = ((), (), s32[]{:S(2)}) async-start(), calls=%async_computation.1 | async-start | bytes 37748736 | tf_op jit(solution)/shard_map/all_gather | solution.py:52
  135.6 0.7 copy-start.3
  135.6 1.0 copy-start.4
Sparse Core Ops, SparseCore 0:
  118.2 337.0 all-gather.2
  456.8 286.2 all-gather.4

commit v2 on v1

v2 whole, which is shorter than its diff:
```python
import functools

import jax
import jax.numpy as jnp
from jax import lax
from jax.experimental import pallas as pl
from jax.experimental.pallas import tpu as pltpu
from jax.sharding import PartitionSpec as P

TILE = 128
EVERY = ("src", "rcv", "int")
MESH = pl.DeviceIdType.MESH
LAG_FILL = 2
LAG_MOVE = 3


def product(left_side, right_side):
    return jnp.dot(left_side, right_side, precision=lax.Precision.HIGH)


def gather_kernel(sizes, own, mask, right, left, turned, kept, recv, recv_turn, sent, local):
    layers, int_count, rows, edge = sizes
    na = rows // edge
    nb = 2 * na
    rounds = na * nb
    s = lax.axis_index("src")
    z, c = s // 2, s % 2
    q = lax.axis_index("rcv") * int_count + lax.axis_index("int")

    def device(layer, core, column):
        return {"src": 2 * layer + core, "rcv": column // int_count, "int": column % int_count}

    def straight(r):
        a, rest = r // nb, r % nb
        return a, na * (rest % 2) + rest // 2

    def mirrored(r):
        a, rest = r // nb, r % nb
        return rest // 2, na * (rest % 2) + a

    def place(layer, column, r):
        (a0, b0), (a1, b1) = straight(r), mirrored(r)
        raw = jnp.where(layer > column, 1, 0)
        return a0 * raw + a1 * (1 - raw), b0 * raw + b1 * (1 - raw)

    def span(index, base=0):
        return pl.ds(pl.multiple_of(base + index * edge, edge), edge)

    def in_right(layer, core, a, b):
        return right.at[:, span(a, (2 * layer + core) * rows), span(b)]

    DOWN, UP, SIDE, ROW, TURN = range(5)

    def remote(source, target, kind, j, r, where, sem=None):
        return pltpu.make_async_remote_copy(
            src_ref=source,
            dst_ref=target,
            send_sem=sent.at[kind, j, r],
            recv_sem=recv.at[kind, j, r] if sem is None else sem,
            device_id=where,
            device_id_type=MESH,
        )

    def move(kind, j, r, source):
        a, b = place(j, q, r)
        where = {DOWN: (z - 1, c), UP: (z + 1, c), SIDE: (z, 1 - c)}[kind]
        source = in_right(j, c, a, b) if source is None else source.at[:, span(a), span(b)]
        return remote(source, in_right(j, c, a, b), kind, j, r, device(*where, q))

    def arrival(kind, j, core, r):
        a, b = place(j, q, r)
        ref = in_right(j, core, a, b)
        return remote(ref, ref, kind, j, r, device(z, 1 - c, q))

    def row_send(other, r):
        a, b = place(z, q, r)
        return remote(
            kept.at[:, span(a), span(b)], left.at[q, :, span(a), span(b)], ROW, other, r, device(z, c, other),
            recv.at[ROW, q, r],
        )

    def row_arrival(other, r):
        a, b = place(z, other, r)
        ref = left.at[other, :, span(a), span(b)]
        return remote(ref, ref, ROW, other, r, device(z, 1 - c, q))

    def turn_parts(j, r, source):
        a, b = straight(r)
        core = b // na
        slot = a * nb + 2 * (b % na) + c
        ref = in_right(j, c, a, b) if source is None else source.at[:, span(a), span(b)]
        return ref, core, slot

    def turn(j, r, source):
        ref, core, slot = turn_parts(j, r, source)
        return remote(ref, turned.at[slot], TURN, j, r, device(z, core, j), recv_turn.at[slot])

    def turn_here(r):
        ref, _, slot = turn_parts(z, r, own)
        return pltpu.make_async_copy(ref, turned.at[slot], recv_turn.at[slot])

    def keep(which, r):
        a, b = place(z, q, r)
        target = in_right(z, c, a, b) if which == 0 else left.at[q, :, span(a), span(b)]
        return pltpu.make_async_copy(kept.at[:, span(a), span(b)], target, local.at[which, r])

    def turn_arrival(f):
        return pltpu.make_async_copy(turned.at[f], turned.at[f], recv_turn.at[f])

    barrier = pltpu.get_barrier_semaphore()

    def greet(layer, core, column):
        pl.semaphore_signal(barrier, inc=1, device_id=device(layer, core, column), device_id_type=MESH)

    for column in range(layers):
        greet(z, 1 - c, column)

        @pl.when(column != q)
        def _():
            greet(z, c, column)

    @pl.when(z > 0)
    def _():
        greet(z - 1, c, q)

    @pl.when(z < layers - 1)
    def _():
        greet(z + 1, c, q)

    ends = jnp.where(z > 0, 1, 0) + jnp.where(z < layers - 1, 1, 0)
    pl.semaphore_wait(barrier, 2 * layers - 1 + ends)

    def own_moves(r, do):
        @pl.when(z > 0)
        def _():
            do(move(DOWN, z, r, kept))

        @pl.when(z < layers - 1)
        def _():
            do(move(UP, z, r, kept))

        do(move(SIDE, z, r, kept))
        for other in range(layers):

            @pl.when(other != q)
            def _():
                do(row_send(other, r))

    def start(copy):
        copy.start()

    def own_round(r):
        a, b = place(z, q, r)

        @pl.when(z > q)
        def _():
            kept[:, span(a), span(b)] = own[:, span(a), span(b)]

        @pl.when(z <= q)
        def _():
            turn_arrival(r).wait()
            per = edge // TILE
            for comp in range(2):
                flipped = turned[r, comp].T
                for i in range(per):
                    row = pl.ds(pl.multiple_of(a * edge + i * TILE, TILE), TILE)
                    marks = mask[pl.ds(pl.multiple_of((a * per + i) * 8, 8), 1), span(b)]
                    part = flipped[i * TILE : (i + 1) * TILE]
                    kept[comp, row, span(b)] = jnp.where(marks > 0.5, part, own[comp, row, span(b)])

        own_moves(r, start)
        keep(0, r).start()
        keep(1, r).start()

    def pass_on(j, r, do, waiting):
        @pl.when(z < j)
        def _():
            if waiting:
                arrival(DOWN, j, c, r).wait_recv()

            @pl.when(z > 0)
            def _():
                do(move(DOWN, j, r, None))

            @pl.when(q == z)
            def _():
                do(turn(j, r, None))

        @pl.when(z > j)
        def _():
            if waiting:
                arrival(UP, j, c, r).wait_recv()

            @pl.when(z < layers - 1)
            def _():
                do(move(UP, j, r, None))

        @pl.when(z != j)
        def _():
            do(move(SIDE, j, r, None))

    def first_turn(r, _):
        @pl.when(straight(r)[1] // na == c)
        def _():
            turn_here(r).start()

        @pl.when(straight(r)[1] // na != c)
        def _():
            turn(z, r, own).start()

        return 0

    @pl.when(q == z)
    def _():
        lax.fori_loop(0, rounds, first_turn, 0)

    def step(t, _):
        @pl.when((t < rounds) & (z > q))
        def _():
            own_round(t)

        @pl.when(t < rounds)
        def _():
            for j in range(layers):

                @pl.when(j > q)
                def _():
                    pass_on(j, t, start, True)

        @pl.when((t >= LAG_FILL) & (t < rounds + LAG_FILL) & (z <= q))
        def _():
            own_round(t - LAG_FILL)

        @pl.when(t >= LAG_MOVE)
        def _():
            for j in range(layers):

                @pl.when(j <= q)
                def _():
                    pass_on(j, t - LAG_MOVE, start, True)

        return 0

    lax.fori_loop(0, rounds + LAG_MOVE, step, 0)

    def done(copy):
        copy.wait_send()

    def finish(r, _):
        own_moves(r, done)
        keep(0, r).wait()
        keep(1, r).wait()
        for j in range(layers):
            pass_on(j, r, done, False)
            arrival(SIDE, j, 1 - c, r).wait_recv()

            @pl.when(j != q)
            def _():
                row_arrival(j, r).wait_recv()

        @pl.when((q == z) & (straight(r)[1] // na != c))
        def _():
            turn(z, r, own).wait_send()

        return 0

    lax.fori_loop(0, rounds, finish, 0)


def gather_panels(own, mask, layers, int_count):
    rows = own.shape[1]
    edge = max(TILE, rows // 2)
    rounds = 2 * (rows // edge) ** 2
    return pl.pallas_call(
        functools.partial(gather_kernel, (layers, int_count, rows, edge)),
        out_shape=(
            jax.ShapeDtypeStruct((2, 2 * layers * rows, 2 * rows), jnp.float32),
            jax.ShapeDtypeStruct((layers, 2, rows, 2 * rows), jnp.float32),
        ),
        in_specs=[pl.BlockSpec(memory_space=pltpu.VMEM)] * 2,
        out_specs=[pl.BlockSpec(memory_space=pl.ANY)] * 2,
        scratch_shapes=[
            pltpu.VMEM((rounds, 2, edge, edge), jnp.float32),
            pltpu.VMEM((2, rows, 2 * rows), jnp.float32),
            pltpu.SemaphoreType.DMA((4, layers, rounds)),
            pltpu.SemaphoreType.DMA((rounds,)),
            pltpu.SemaphoreType.DMA((5, layers, rounds)),
            pltpu.SemaphoreType.DMA((2, rounds)),
        ],
        compiler_params=pltpu.CompilerParams(
            collective_id=0, has_side_effects=True, vmem_limit_bytes=40 * 2**20
        ),
    )(own, mask)


def per_device(traces, missing, aperture, wavelet):
    src_count, rcv_count, int_count = (lax.axis_size(a) for a in EVERY)
    col_count = rcv_count * int_count
    assert src_count == 2 * col_count
    rows, wide = traces.shape[2], traces.shape[3]
    cols = wide // int_count
    my_int = lax.axis_index("int")
    s = lax.axis_index("src")
    own = lax.dynamic_slice_in_dim(traces[:, 0], my_int * cols, cols, axis=2)
    row_tiles, col_tiles = rows // TILE, cols // TILE
    my_missing = lax.dynamic_slice_in_dim(missing, my_int * col_tiles, col_tiles, axis=1)
    mask = jnp.repeat(jnp.repeat((my_missing > 0).astype(jnp.float32), 8, axis=0), TILE, axis=1)
    right, left = gather_panels(own, mask, col_count, int_count)
    filled = lax.dynamic_slice_in_dim(right, s * rows, rows, axis=1)
    blocks = col_count * col_tiles
    chosen = (
        (aperture[:, :, None] == jnp.arange(blocks, dtype=jnp.int32)[None, None, :])
        .astype(jnp.float32)
        .sum(axis=1)
    )
    scale = jnp.repeat(jnp.repeat(chosen, TILE, axis=0), TILE, axis=1)
    left = jnp.moveaxis(left, 0, 2).reshape(2, rows, col_count * cols) * scale[None]
    first_prod = product(left[0], right[0])
    second_prod = product(left[1], right[1])
    third_prod = product(left[0] + left[1], right[0] + right[1])
    real = first_prod - second_prod
    imag = third_prod - first_prod - second_prod
    w_real, w_imag = wavelet[0, 0], wavelet[1, 0]
    out_real = filled[0] - (w_real * real - w_imag * imag)
    out_imag = filled[1] - (w_real * imag + w_imag * real)
    return jnp.stack([out_real, out_imag])[:, None]


def solution(mesh):
    placed = (P(None, None, "src", "rcv"), P("src", "rcv"), P("src", None), P())
    return jax.shard_map(
        per_device,
        mesh=mesh,
        in_specs=placed,
        out_specs=P(None, None, "src", ("rcv", "int")),
        check_vma=False,
    )
```

time: 841 us -> 560 us (0.67)
  waiting for transfers between devices: 645 us -> 0 us
  Pallas kernels: 0 us -> 437 us
  local copies, waits for them, and re-layouts: 48.3 us -> 25.7 us
  other arithmetic: 36.5 us -> 16.3 us
  between operations: 13.5 us -> 0.07 us
  starting transfers between devices: 10.5 us -> 0 us
    all_gather x2 -> x0, waiting for transfers between devices: 575 us -> none  [the longest x1 318 us: per_device(): left = lax.all_gather(filled, ('rcv', 'int'), axis=0)]
    pallas_call x0 -> x1, Pallas kernels: none -> 437 us  [gather_panels(): pl.pallas_call(functools.partial(gather_kernel, (layers, int_count, rows,...]
    ppermute x4 -> x0, waiting for transfers between devices: 70.2 us -> none  [per_device(): arrived.append(lax.ppermute(part, EVERY, pairs))]
    all_gather x1 -> x0, local copies, waits for them, and re-layouts: 17.2 us -> none  [per_device(): left = lax.all_gather(filled, ('rcv', 'int'), axis=0)]
    transpose x0 -> x1, local copies, waits for them, and re-layouts: none -> 16.6 us  [per_device(): jnp.moveaxis(left, 0, 2).reshape(2, rows, col_count * cols) * scale[None]]
    ppermute x4 -> x0, starting transfers between devices: 10.3 us -> none  [per_device(): arrived.append(lax.ppermute(part, EVERY, pairs))]
    select_n x2 -> x0, other arithmetic: 10.1 us -> none  [per_device(): filled = jnp.where(mask[None], mirrored, own)]
    concatenate x3 -> x0, other arithmetic: 9.56 us -> none  [per_device(): jnp.concatenate([jnp.swapaxes(first, 1, 2), jnp.swapaxes(second, 1, 2)],...]
  transfers between devices with their start and end apart: 6 -> 0, of which waited for: 4 -> 0; matrix products, arithmetic and copies ran while one was open for 7% -> 0% of each run, Pallas kernels for 0% -> 0%
where the time goes in v2:
time: 560 us; the launch traced here: 559 us
  Pallas kernels  437 us (78%)
  matrix products  80.6 us (14%)
  local copies, waits for them, and re-layouts  25.7 us (5%)
  other arithmetic  16.3 us (3%)
    pallas_call x1, Pallas kernels, gather_panels(): pl.pallas_call(functools.partial(gather_kernel, (layers, int_count, rows,...  437 us
    dot_general x3, matrix products, product(): return jnp.dot(left_side, right_side, precision=lax.Precision.HIGH)  80.6 us
    transpose x1, local copies, waits for them, and re-layouts, per_device(): jnp.moveaxis(left, 0, 2).reshape(2, rows, col_count * cols) * scale[None]  16.6 us
    mul x1, other arithmetic, per_device(): jnp.moveaxis(left, 0, 2).reshape(2, rows, col_count * cols) * scale[None]  12.1 us

profile of v2, /device:TPU:29, one launch (start us, length us, event | category | flops | bytes accessed | tf_op | source)
XLA Modules:
  0.0 559.2 jit_solution(5606955972857971783)
XLA Ops:
  0.0 0.0 copy-start.1
  0.0 4.8 dynamic-slice_bitcast_fusion.own
  4.8 0.0 copy-done.1
  4.8 0.1 fusion.27
  4.9 0.1 broadcast_in_dim.18
  5.0 0.0 copy-start
  5.0 2.2 copy-done
  7.2 436.6 %shard_map.46 = (f32[2,4096,1024]{2,1,0:T(8,128)}, f32[4,2,512,1024]{3,2,1,0:T(8,128)}) custom-call(f32[2,512,1024]{2,1,0:T(8,128)S(1)} %copy-done, f32[32,1024]{1,0:T(8,128)S(1)} %bitcast.66), custom_call_target="tpu_custom_call" | custom-call | tf_op jit(solution)/shard_map/pallas_call | solution.py:274
  443.8 0.0 copy-start.2
  443.8 16.6 %copy.8 = f32[2,512,4,1024]{1,3,2,0:T(8,128)} copy(f32[2,512,4,1024]{3,1,0,2:T(8,128)} %bitcast.68) | data formatting | bytes 33554432 | tf_op jit(solution)/shard_map/transpose | solution.py:317
  460.4 0.0 copy-done.2
  460.4 0.1 convert_reduce_fusion
  460.5 0.1 copy.9
  460.6 0.1 broadcast_in_dim.19
  460.7 1.1 broadcast_in_dim.20
  461.8 12.1 %bitcast_multiply_fusion = f32[2,512,4096]{1,2,0:T(8,128)} fusion(f32[2,512,4,1024]{1,3,2,0:T(8,128)} %copy.8, f32[512,4096]{0,1:T(8,128)S(1)} %bitcast.67), kind=kLoop, calls=%fused_computation.6 | loop fusion | flops 4194304 | bytes 41943040 | tf_op jit(solution)/shard_map/mul | solution.py:317
  473.9 19.7 %fusion.2 = f32[512,1024]{1,0:T(8,128)} fusion(f32[2,4096,1024]{2,1,0:T(8,128)} %get-tuple-element.7, f32[2,512,4096]{1,2,0:T(8,128)} %bitcast_multiply_fusion), kind=kOutput, calls=%fused_computation.2 | convolution fusion | flops 12884901888 | bytes 27262976 | tf_op jit(solution)/shard_map/dot_general | solution.py:18
  493.7 0.0 copy-start.3
  493.7 19.7 %fusion.4 = f32[512,1024]{1,0:T(8,128)} fusion(f32[2,4096,1024]{2,1,0:T(8,128)} %get-tuple-element.7, f32[2,512,4096]{1,2,0:T(8,128)} %bitcast_multiply_fusion), kind=kOutput, calls=%fused_computation.4 | convolution fusion | flops 12884901888 | bytes 27262976 | tf_op jit(solution)/shard_map/dot_general | solution.py:18
  513.4 0.0 copy-done.3
  513.4 0.7 fusion.28
  514.0 41.1 %fusion.22 = (f32[1,512,1024]{2,1,0:T(8,128)S(1)}, f32[1,512,1024]{2,1,0:T(8,128)}) fusion(f32[2,4096,1024]{2,1,0:T(8,128)} %get-tuple-element.7, s32[]{:T(128)S(6)} %select_n.11, f32[]{:T(128)} %bitcast.11, f32[]{:T(128)} %bitcast.3, f32[512,1024]{1,0:T(8,128)} %fusion.4, f32[512,1024]{1,0:T(8,128)} %fusion.2, s32[]{:T(128)S(6)} %add.32, ...), kind=kOutput, calls=%fused_computation.27 | convolution fusion | flops 12896960512 | bytes 62915592 | tf_op jit(solution)/shard_map/dot_general | solution.py:18
  555.1 4.0 maximum_bitcast_fusion
  (3 shorter events, 0.0 us)
Async XLA Ops:
  0.0 4.8 copy-start.1
  5.0 2.2 copy-start
  443.8 16.7 %copy-start.2 = (s32[4,24]{1,0:T(4,128)S(1)}, s32[4,24]{1,0:T(4,128)}, u32[]{:S(2)}) copy-start(s32[4,24]{1,0:T(4,128)} %param.6) | copy-start | bytes 1156
  493.7 19.7 %copy-start.3 = (f32[2,1]{0,1:T(1,128)S(1)}, f32[2,1]{0,1:T(1,128)}, u32[]{:S(2)}) copy-start(f32[2,1]{0,1:T(1,128)} %param.7) | copy-start | bytes 28

commit v3 on v2

--- a/solution.py
+++ b/solution.py
@@ -10,12 +10,64 @@
 TILE = 128
 EVERY = ("src", "rcv", "int")
 MESH = pl.DeviceIdType.MESH
-LAG_FILL = 2
-LAG_MOVE = 3
-
-
-def product(left_side, right_side):
-    return jnp.dot(left_side, right_side, precision=lax.Precision.HIGH)
+LAG_FILL = 4
+LAG_MOVE = 6
+
+
+def split(value):
+    high = value.astype(jnp.bfloat16)
+    return high, (value - high.astype(jnp.float32)).astype(jnp.bfloat16)
+
+
+def three_pass(left_parts, right_parts):
+    (lh, ll), (rh, rl) = left_parts, right_parts
+    dot = functools.partial(jnp.dot, preferred_element_type=jnp.float32)
+    return dot(lh, rh) + (dot(lh, rl) + dot(ll, rh))
+
+
+def predict_kernel(left, right, scale, kept, wavelet, out, total):
+    step = pl.program_id(1)
+
+    @pl.when(step == 0)
+    def _():
+        total[...] = jnp.zeros_like(total)
+
+    weights = scale[...]
+    lr, li = left[0] * weights, left[1] * weights
+    fr, fi = right[0], right[1]
+    first = three_pass(split(lr), split(fr))
+    second = three_pass(split(li), split(fi))
+    total[0] += first - second
+    total[1] += three_pass(split(lr + li), split(fr + fi)) - (first + second)
+
+    @pl.when(step == pl.num_programs(1) - 1)
+    def _():
+        wr, wi = wavelet[0, 0], wavelet[1, 0]
+        out[0] = kept[0] - (wr * total[0] - wi * total[1])
+        out[1] = kept[1] - (wr * total[1] + wi * total[0])
+
+
+def predict(left, right, scale, wavelet, place):
+    blocks, _, rows, wide = left.shape
+    cols = right.shape[2]
+    deep = min(wide, 512)
+    per = wide // deep
+    width = min(cols, 512)
+    return pl.pallas_call(
+        predict_kernel,
+        grid=(cols // width, blocks * per),
+        in_specs=[
+            pl.BlockSpec((None, 2, rows, deep), lambda n, k: (k // per, 0, 0, k % per)),
+            pl.BlockSpec((2, deep, width), lambda n, k: (0, k, n)),
+            pl.BlockSpec((rows, deep), lambda n, k: (0, k)),
+            pl.BlockSpec((2, rows, width), lambda n, k: (0, 0, n)),
+            pl.BlockSpec(memory_space=pltpu.SMEM),
+        ],
+        out_specs=pl.BlockSpec((2, rows, width), lambda n, k: (0, 0, n)),
+        out_shape=jax.ShapeDtypeStruct((2, rows, cols), jnp.float32),
+        scratch_shapes=[pltpu.VMEM((2, rows, width), jnp.float32)],
+        compiler_params=pltpu.CompilerParams(vmem_limit_bytes=56 * 2**20),
+    )(left, right, scale, place, wavelet)
 
 
 def gather_kernel(sizes, own, mask, right, left, turned, kept, recv, recv_turn, sent, local):
@@ -25,7 +77,8 @@
     rounds = na * nb
     s = lax.axis_index("src")
     z, c = s // 2, s % 2
-    q = lax.axis_index("rcv") * int_count + lax.axis_index("int")
+    y, x = lax.axis_index("rcv"), lax.axis_index("int")
+    q = y * int_count + x
 
     def device(layer, core, column):
         return {"src": 2 * layer + core, "rcv": column // int_count, "int": column % int_count}
@@ -49,7 +102,7 @@
     def in_right(layer, core, a, b):
         return right.at[:, span(a, (2 * layer + core) * rows), span(b)]
 
-    DOWN, UP, SIDE, ROW, TURN = range(5)
+    DOWN, UP, SIDE, ROW, TURN, RELAY = range(6)
 
     def remote(source, target, kind, j, r, where, sem=None):
         return pltpu.make_async_remote_copy(
@@ -84,6 +137,23 @@
         ref = left.at[other, :, span(a), span(b)]
         return remote(ref, ref, ROW, other, r, device(z, 1 - c, q))
 
+    def relays(r, do, waiting):
+        for other in range(layers):
+
+            @pl.when((other != q) & (other % int_count == x))
+            def _():
+                if waiting:
+                    row_arrival(other, r).wait_recv()
+                a, b = place(z, other, r)
+                ref = left.at[other, :, span(a), span(b)]
+                for x2 in range(int_count):
+
+                    @pl.when(x2 != x)
+                    def _():
+                        to = (other // int_count) * int_count + x2
+                        where = device(z, c, y * int_count + x2)
+                        do(remote(ref, ref, RELAY, to, r, where, recv.at[ROW, other, r]))
+
     def turn_parts(j, r, source):
         a, b = straight(r)
         core = b // na
@@ -142,7 +212,7 @@
         do(move(SIDE, z, r, kept))
         for other in range(layers):
 
-            @pl.when(other != q)
+            @pl.when((other != q) & ((other % int_count == x) | (other // int_count == y)))
             def _():
                 do(row_send(other, r))
 
@@ -239,6 +309,8 @@
                 def _():
                     pass_on(j, t - LAG_MOVE, start, True)
 
+            relays(t - LAG_MOVE, start, True)
+
         return 0
 
     lax.fori_loop(0, rounds + LAG_MOVE, step, 0)
@@ -248,13 +320,14 @@
 
     def finish(r, _):
         own_moves(r, done)
+        relays(r, done, False)
         keep(0, r).wait()
         keep(1, r).wait()
         for j in range(layers):
             pass_on(j, r, done, False)
             arrival(SIDE, j, 1 - c, r).wait_recv()
 
-            @pl.when(j != q)
+            @pl.when((j != q) & (j % int_count != x))
             def _():
                 row_arrival(j, r).wait_recv()
 
@@ -269,7 +342,7 @@
 
 def gather_panels(own, mask, layers, int_count):
     rows = own.shape[1]
-    edge = max(TILE, rows // 2)
+    edge = max(TILE, rows // 4)
     rounds = 2 * (rows // edge) ** 2
     return pl.pallas_call(
         functools.partial(gather_kernel, (layers, int_count, rows, edge)),
@@ -284,7 +357,7 @@
             pltpu.VMEM((2, rows, 2 * rows), jnp.float32),
             pltpu.SemaphoreType.DMA((4, layers, rounds)),
             pltpu.SemaphoreType.DMA((rounds,)),
-            pltpu.SemaphoreType.DMA((5, layers, rounds)),
+            pltpu.SemaphoreType.DMA((6, layers, rounds)),
             pltpu.SemaphoreType.DMA((2, rounds)),
         ],
         compiler_params=pltpu.CompilerParams(
@@ -314,16 +387,7 @@
         .sum(axis=1)
     )
     scale = jnp.repeat(jnp.repeat(chosen, TILE, axis=0), TILE, axis=1)
-    left = jnp.moveaxis(left, 0, 2).reshape(2, rows, col_count * cols) * scale[None]
-    first_prod = product(left[0], right[0])
-    second_prod = product(left[1], right[1])
-    third_prod = product(left[0] + left[1], right[0] + right[1])
-    real = first_prod - second_prod
-    imag = third_prod - first_prod - second_prod
-    w_real, w_imag = wavelet[0, 0], wavelet[1, 0]
-    out_real = filled[0] - (w_real * real - w_imag * imag)
-    out_imag = filled[1] - (w_real * imag + w_imag * real)
-    return jnp.stack([out_real, out_imag])[:, None]
+    return predict(left, right, scale, wavelet, filled)[:, None]
 
 
 def solution(mesh):

time: 560 us -> 717 us (1.28); the launches traced: 559 us -> 706 us
  Pallas kernels: 437 us -> 682 us
  matrix products: 80.6 us -> 0 us
  other arithmetic: 16.3 us -> 1.52 us
    pallas_call x1, Pallas kernels: 437 us -> 632 us  [gather_panels(): pl.pallas_call(functools.partial(gather_kernel, (layers, int_count, rows,...]
    dot_general x3 -> x0, matrix products: 80.6 us -> none  [product(): return jnp.dot(left_side, right_side, precision=lax.Precision.HIGH)]
    pallas_call x0 -> x1, Pallas kernels: none -> 50.7 us  [predict(): pl.pallas_call(predict_kernel, grid=(cols // width, blocks * per), in_spe...]
    transpose x1 -> x0, local copies, waits for them, and re-layouts: 16.6 us -> none  [per_device(): jnp.moveaxis(left, 0, 2).reshape(2, rows, col_count * cols) * scale[None]]
    mul x1 -> x0, other arithmetic: 12.1 us -> none  [per_device(): jnp.moveaxis(left, 0, 2).reshape(2, rows, col_count * cols) * scale[None]]
    unnamed x10 -> x3, local copies, waits for them, and re-layouts: 2.23 us -> 12.6 us
where the time goes in v3:
time: 717 us; the launch traced here: 706 us
  Pallas kernels  682 us (95%)
  local copies, waits for them, and re-layouts  22.2 us (3%)
    pallas_call x1, Pallas kernels, gather_panels(): pl.pallas_call(functools.partial(gather_kernel, (layers, int_count, rows,...  632 us
    pallas_call x1, Pallas kernels, predict(): pl.pallas_call(predict_kernel, grid=(cols // width, blocks * per), in_spe...  50.7 us

profile of v3, /device:TPU:29, one launch (start us, length us, event | category | flops | bytes accessed | tf_op | source)
XLA Modules:
  0.0 706.2 jit_solution(14790145533634627869)
XLA Ops:
  0.0 1.3 copy.7.wavelet
  1.3 0.8 fusion
  2.0 0.8 convert_reduce_fusion
  2.8 0.1 broadcast_in_dim.18
  3.0 2.5 dynamic-slice_bitcast_fusion.own
  5.5 2.3 broadcast_in_dim.20
  7.8 11.3 %copy.13 = f32[64,8,32,128]{3,1,2,0:T(8,128)} copy(f32[64,8,32,128]{3,2,1,0:T(8,128)S(1)} %bitcast.18) | data formatting | bytes 16777216
  19.1 631.7 %shard_map.46 = (f32[2,4096,1024]{2,1,0:T(8,128)}, f32[4,2,512,1024]{3,2,1,0:T(8,128)}) custom-call(f32[2,512,1024]{2,1,0:T(8,128)S(1)} %dynamic-slice_bitcast_fusion.own, f32[32,1024]{1,0:T(8,128)S(1)} %bitcast.16), custom_call_target="tpu_custom_call" | custom-call | tf_op jit(solution)/shard_map/pallas_call | solution.py:347
  650.8 4.7 constant_dynamic-slice_fusion.kept
  655.5 50.7 %shard_map.47 = f32[2,512,1024]{2,1,0:T(8,128)} custom-call(f32[4,2,512,1024]{3,2,1,0:T(8,128)} %get-tuple-element.7.left, f32[2,4096,1024]{2,1,0:T(8,128)} %get-tuple-element.8.right, f32[512,4096]{1,0:T(8,128)} %bitcast.17, f32[2,512,1024]{2,1,0:T(8,128)} %constant_dynamic-slice_fusion.kept, f32[2,1]{1,0:T(2,128)} %copy.7.wavelet), custom_call_target="tpu_custom_call" | custom-call | tf_op jit(solution)/shard_map/pallas_call | solution.py:56
  (3 shorter events, 0.0 us)

commit v4 on v3

--- a/solution.py
+++ b/solution.py
@@ -10,8 +10,8 @@
 TILE = 128
 EVERY = ("src", "rcv", "int")
 MESH = pl.DeviceIdType.MESH
-LAG_FILL = 4
-LAG_MOVE = 6
+LAG_FILL = 2
+LAG_MOVE = 3
 
 
 def split(value):
@@ -25,16 +25,34 @@
     return dot(lh, rh) + (dot(lh, rl) + dot(ll, rh))
 
 
-def predict_kernel(left, right, scale, kept, wavelet, out, total):
+def predict_kernel(my_block, left, right, chosen, kept, wavelet, out, total):
     step = pl.program_id(1)
+    na, _, _, edge, _ = left.shape
+    nb = right.shape[1]
+    per = edge // TILE
 
     @pl.when(step == 0)
     def _():
         total[...] = jnp.zeros_like(total)
 
-    weights = scale[...]
-    lr, li = left[0] * weights, left[1] * weights
-    fr, fi = right[0], right[1]
+    def weighted(comp):
+        bands = []
+        for a in range(na):
+            for i in range(per):
+                tiles = []
+                for b in range(na):
+                    for k in range(per):
+                        tile = left[a, b, comp, i * TILE : (i + 1) * TILE, k * TILE : (k + 1) * TILE]
+                        tiles.append(tile * chosen[a * per + i, (step * na + b) * per + k])
+                bands.append(jnp.concatenate(tiles, axis=1))
+        return jnp.concatenate(bands, axis=0)
+
+    def panel(comp):
+        bands = [jnp.concatenate([right[a, b, comp] for b in range(nb)], axis=1) for a in range(na)]
+        return jnp.concatenate(bands, axis=0)
+
+    lr, li = weighted(0), weighted(1)
+    fr, fi = panel(0), panel(1)
     first = three_pass(split(lr), split(fr))
     second = three_pass(split(li), split(fi))
     total[0] += first - second
@@ -43,31 +61,42 @@
     @pl.when(step == pl.num_programs(1) - 1)
     def _():
         wr, wi = wavelet[0, 0], wavelet[1, 0]
-        out[0] = kept[0] - (wr * total[0] - wi * total[1])
-        out[1] = kept[1] - (wr * total[1] + wi * total[0])
-
-
-def predict(left, right, scale, wavelet, place):
-    blocks, _, rows, wide = left.shape
-    cols = right.shape[2]
-    deep = min(wide, 512)
-    per = wide // deep
+        for a in range(na):
+            for b in range(nb):
+                at = (slice(a * edge, (a + 1) * edge), slice(b * edge, (b + 1) * edge))
+                real, imag = total[0, *at], total[1, *at]
+                out[0, *at] = kept[a, b, 0] - (wr * real - wi * imag)
+                out[1, *at] = kept[a, b, 1] - (wr * imag + wi * real)
+
+
+def predict(left, right, chosen, wavelet, my_block, na):
+    columns, rounds, _, edge, _ = left.shape
+    blocks = right.shape[0]
+    nb = rounds // na
+    left = left.reshape(columns, na, nb, 2, edge, edge)
+    right = right.reshape(blocks, na, nb, 2, edge, edge)
+    rows, cols = na * edge, nb * edge
     width = min(cols, 512)
+    some = width // edge
+    panel = (None, na, some, 2, edge, edge)
     return pl.pallas_call(
         predict_kernel,
-        grid=(cols // width, blocks * per),
-        in_specs=[
-            pl.BlockSpec((None, 2, rows, deep), lambda n, k: (k // per, 0, 0, k % per)),
-            pl.BlockSpec((2, deep, width), lambda n, k: (0, k, n)),
-            pl.BlockSpec((rows, deep), lambda n, k: (0, k)),
-            pl.BlockSpec((2, rows, width), lambda n, k: (0, 0, n)),
-            pl.BlockSpec(memory_space=pltpu.SMEM),
-        ],
-        out_specs=pl.BlockSpec((2, rows, width), lambda n, k: (0, 0, n)),
+        grid_spec=pltpu.PrefetchScalarGridSpec(
+            num_scalar_prefetch=1,
+            grid=(cols // width, blocks),
+            in_specs=[
+                pl.BlockSpec((None, na, na, 2, edge, edge), lambda n, k, s: (k // 2, 0, k % 2, 0, 0, 0)),
+                pl.BlockSpec(panel, lambda n, k, s: (k, 0, n, 0, 0, 0)),
+                pl.BlockSpec(memory_space=pltpu.SMEM),
+                pl.BlockSpec(panel, lambda n, k, s: (s[0], 0, n, 0, 0, 0)),
+                pl.BlockSpec(memory_space=pltpu.SMEM),
+            ],
+            out_specs=pl.BlockSpec((2, rows, width), lambda n, k, s: (0, 0, n)),
+            scratch_shapes=[pltpu.VMEM((2, rows, width), jnp.float32)],
+        ),
         out_shape=jax.ShapeDtypeStruct((2, rows, cols), jnp.float32),
-        scratch_shapes=[pltpu.VMEM((2, rows, width), jnp.float32)],
         compiler_params=pltpu.CompilerParams(vmem_limit_bytes=56 * 2**20),
-    )(left, right, scale, place, wavelet)
+    )(my_block, left, right, chosen, right, wavelet)
 
 
 def gather_kernel(sizes, own, mask, right, left, turned, kept, recv, recv_turn, sent, local):
@@ -96,11 +125,8 @@
         raw = jnp.where(layer > column, 1, 0)
         return a0 * raw + a1 * (1 - raw), b0 * raw + b1 * (1 - raw)
 
-    def span(index, base=0):
-        return pl.ds(pl.multiple_of(base + index * edge, edge), edge)
-
     def in_right(layer, core, a, b):
-        return right.at[:, span(a, (2 * layer + core) * rows), span(b)]
+        return right.at[2 * layer + core, a * nb + b]
 
     DOWN, UP, SIDE, ROW, TURN, RELAY = range(6)
 
@@ -117,7 +143,7 @@
     def move(kind, j, r, source):
         a, b = place(j, q, r)
         where = {DOWN: (z - 1, c), UP: (z + 1, c), SIDE: (z, 1 - c)}[kind]
-        source = in_right(j, c, a, b) if source is None else source.at[:, span(a), span(b)]
+        source = in_right(j, c, a, b) if source is None else source.at[a * nb + b]
         return remote(source, in_right(j, c, a, b), kind, j, r, device(*where, q))
 
     def arrival(kind, j, core, r):
@@ -128,13 +154,13 @@
     def row_send(other, r):
         a, b = place(z, q, r)
         return remote(
-            kept.at[:, span(a), span(b)], left.at[q, :, span(a), span(b)], ROW, other, r, device(z, c, other),
+            kept.at[a * nb + b], left.at[q, a * nb + b], ROW, other, r, device(z, c, other),
             recv.at[ROW, q, r],
         )
 
     def row_arrival(other, r):
         a, b = place(z, other, r)
-        ref = left.at[other, :, span(a), span(b)]
+        ref = left.at[other, a * nb + b]
         return remote(ref, ref, ROW, other, r, device(z, 1 - c, q))
 
     def relays(r, do, waiting):
@@ -145,7 +171,7 @@
                 if waiting:
                     row_arrival(other, r).wait_recv()
                 a, b = place(z, other, r)
-                ref = left.at[other, :, span(a), span(b)]
+                ref = left.at[other, a * nb + b]
                 for x2 in range(int_count):
 
                     @pl.when(x2 != x)
@@ -158,7 +184,7 @@
         a, b = straight(r)
         core = b // na
         slot = a * nb + 2 * (b % na) + c
-        ref = in_right(j, c, a, b) if source is None else source.at[:, span(a), span(b)]
+        ref = in_right(j, c, a, b) if source is None else source.at[a * nb + b]
         return ref, core, slot
 
     def turn(j, r, source):
@@ -171,8 +197,8 @@
 
     def keep(which, r):
         a, b = place(z, q, r)
-        target = in_right(z, c, a, b) if which == 0 else left.at[q, :, span(a), span(b)]
-        return pltpu.make_async_copy(kept.at[:, span(a), span(b)], target, local.at[which, r])
+        target = in_right(z, c, a, b) if which == 0 else left.at[q, a * nb + b]
+        return pltpu.make_async_copy(kept.at[a * nb + b], target, local.at[which, r])
 
     def turn_arrival(f):
         return pltpu.make_async_copy(turned.at[f], turned.at[f], recv_turn.at[f])
@@ -222,21 +248,23 @@
     def own_round(r):
         a, b = place(z, q, r)
 
+        square = a * nb + b
+
         @pl.when(z > q)
         def _():
-            kept[:, span(a), span(b)] = own[:, span(a), span(b)]
+            kept[square] = own[square]
 
         @pl.when(z <= q)
         def _():
             turn_arrival(r).wait()
             per = edge // TILE
+            lanes = pl.ds(pl.multiple_of(b * edge, edge), edge)
             for comp in range(2):
                 flipped = turned[r, comp].T
                 for i in range(per):
-                    row = pl.ds(pl.multiple_of(a * edge + i * TILE, TILE), TILE)
-                    marks = mask[pl.ds(pl.multiple_of((a * per + i) * 8, 8), 1), span(b)]
-                    part = flipped[i * TILE : (i + 1) * TILE]
-                    kept[comp, row, span(b)] = jnp.where(marks > 0.5, part, own[comp, row, span(b)])
+                    row = slice(i * TILE, (i + 1) * TILE)
+                    marks = mask[pl.ds(pl.multiple_of((a * per + i) * 8, 8), 1), lanes]
+                    kept[square, comp, row] = jnp.where(marks > 0.5, flipped[row], own[square, comp, row])
 
         own_moves(r, start)
         keep(0, r).start()
@@ -341,20 +369,19 @@
 
 
 def gather_panels(own, mask, layers, int_count):
-    rows = own.shape[1]
-    edge = max(TILE, rows // 4)
-    rounds = 2 * (rows // edge) ** 2
+    rounds, _, edge, _ = own.shape
+    rows = edge * int((rounds // 2) ** 0.5)
     return pl.pallas_call(
         functools.partial(gather_kernel, (layers, int_count, rows, edge)),
         out_shape=(
-            jax.ShapeDtypeStruct((2, 2 * layers * rows, 2 * rows), jnp.float32),
-            jax.ShapeDtypeStruct((layers, 2, rows, 2 * rows), jnp.float32),
+            jax.ShapeDtypeStruct((2 * layers, *own.shape), jnp.float32),
+            jax.ShapeDtypeStruct((layers, *own.shape), jnp.float32),
         ),
         in_specs=[pl.BlockSpec(memory_space=pltpu.VMEM)] * 2,
         out_specs=[pl.BlockSpec(memory_space=pl.ANY)] * 2,
         scratch_shapes=[
-            pltpu.VMEM((rounds, 2, edge, edge), jnp.float32),
-            pltpu.VMEM((2, rows, 2 * rows), jnp.float32),
+            pltpu.VMEM(own.shape, jnp.float32),
+            pltpu.VMEM(own.shape, jnp.float32),
             pltpu.SemaphoreType.DMA((4, layers, rounds)),
             pltpu.SemaphoreType.DMA((rounds,)),
             pltpu.SemaphoreType.DMA((6, layers, rounds)),
@@ -378,16 +405,19 @@
     row_tiles, col_tiles = rows // TILE, cols // TILE
     my_missing = lax.dynamic_slice_in_dim(missing, my_int * col_tiles, col_tiles, axis=1)
     mask = jnp.repeat(jnp.repeat((my_missing > 0).astype(jnp.float32), 8, axis=0), TILE, axis=1)
+    edge = max(TILE, rows // 2)
+    na = rows // edge
+    own = jnp.stack(
+        [own[:, a * edge : (a + 1) * edge, b * edge : (b + 1) * edge] for a in range(na) for b in range(2 * na)]
+    )
     right, left = gather_panels(own, mask, col_count, int_count)
-    filled = lax.dynamic_slice_in_dim(right, s * rows, rows, axis=1)
     blocks = col_count * col_tiles
     chosen = (
         (aperture[:, :, None] == jnp.arange(blocks, dtype=jnp.int32)[None, None, :])
         .astype(jnp.float32)
         .sum(axis=1)
     )
-    scale = jnp.repeat(jnp.repeat(chosen, TILE, axis=0), TILE, axis=1)
-    return predict(left, right, scale, wavelet, filled)[:, None]
+    return predict(left, right, chosen, wavelet, s.reshape(1), na)[:, None]
 
 
 def solution(mesh):

time: 717 us -> 501 us (0.70)
  Pallas kernels: 682 us -> 488 us
  local copies, waits for them, and re-layouts: 22.2 us -> 7.73 us
    pallas_call x1, Pallas kernels: 632 us -> 438 us  [gather_panels(): pl.pallas_call(functools.partial(gather_kernel, (layers, int_count, rows,...]
    unnamed x3 -> x19, local copies, waits for them, and re-layouts: 12.6 us -> 5.1 us
where the time goes in v4:
time: 501 us; the launch traced here: 496 us
  Pallas kernels  488 us (97%)
  local copies, waits for them, and re-layouts  7.73 us (2%)
    pallas_call x1, Pallas kernels, gather_panels(): pl.pallas_call(functools.partial(gather_kernel, (layers, int_count, rows,...  438 us
    pallas_call x1, Pallas kernels, predict(): pl.pallas_call(predict_kernel, grid_spec=pltpu.PrefetchScalarGridSpec(num...  49.9 us

profile of v4, /device:TPU:29, one launch (start us, length us, event | category | flops | bytes accessed | tf_op | source)
XLA Modules:
  0.0 496.4 jit_solution(745365422573132342)
XLA Ops:
  0.0 2.5 dynamic-slice_bitcast_fusion
  2.5 0.0 copy-start.2
  2.7 0.0 copy-start.3
  2.7 0.0 copy-start.4
  2.9 0.0 copy-start
  2.9 2.0 copy-done
  4.9 0.0 copy-done.2
  4.9 0.1 fusion.8
  5.0 0.1 broadcast_in_dim.12
  5.1 0.0 copy-start.1
  5.1 2.2 copy-done.1
  7.3 437.9 %shard_map.46 = (f32[8,8,2,256,256]{4,3,2,1,0:T(8,128)}, f32[4,8,2,256,256]{4,3,2,1,0:T(8,128)}) custom-call(f32[8,2,256,256]{3,2,1,0:T(8,128)S(1)} %copy-done.1, f32[32,1024]{1,0:T(8,128)S(1)} %bitcast.46), custom_call_target="tpu_custom_call" | custom-call | tf_op jit(solution)/shard_map/pallas_call | solution.py:374
  445.2 0.0 copy-done.3
  445.2 0.6 convert_reduce_fusion.chosen
  445.9 0.0 copy-done.4
  445.9 0.6 copy.7.wavelet
  446.5 49.9 %shard_map.47 = f32[2,512,1024]{2,1,0:T(8,128)} custom-call(s32[1]{0:T(128)} %bitcast.my_block, f32[4,2,4,2,256,256]{5,4,3,2,1,0:T(8,128)} %bitcast.49, f32[8,2,4,2,256,256]{5,4,3,2,1,0:T(8,128)} %bitcast.47, f32[4,32]{1,0:T(4,128)} %convert_reduce_fusion.chosen, f32[8,2,4,2,256,256]{5,4,3,2,1,0:T(8,128)} %bitcast.48, f32[2,1]{1,0:T(2,128)} %copy.7.wavelet), custom_call_target="tpu_custom_call" | custom-call | tf_op jit(solution)/shard_map/pallas_call | solution.py:82
  (10 shorter events, 0.3 us)
Async XLA Ops:
  2.5 2.4 copy-start.2
  2.7 442.5 %copy-start.3 = (s32[4,24]{1,0:T(4,128)S(1)}, s32[4,24]{1,0:T(4,128)}, u32[]{:S(2)}) copy-start(s32[4,24]{1,0:T(4,128)} %param.6) | copy-start | bytes 1156
  2.7 443.1 %copy-start.4 = (f32[2,1]{0,1:T(1,128)S(1)}, f32[2,1]{0,1:T(1,128)}, u32[]{:S(2)}) copy-start(f32[2,1]{0,1:T(1,128)} %param.7) | copy-start | bytes 28
  2.9 2.0 copy-start
  5.1 2.2 copy-start.1

commit v5 on v4

--- a/solution.py
+++ b/solution.py
@@ -10,8 +10,8 @@
 TILE = 128
 EVERY = ("src", "rcv", "int")
 MESH = pl.DeviceIdType.MESH
-LAG_FILL = 2
-LAG_MOVE = 3
+LAG_FILL = 4
+LAG_MOVE = 7
 
 
 def split(value):
@@ -405,7 +405,7 @@
     row_tiles, col_tiles = rows // TILE, cols // TILE
     my_missing = lax.dynamic_slice_in_dim(missing, my_int * col_tiles, col_tiles, axis=1)
     mask = jnp.repeat(jnp.repeat((my_missing > 0).astype(jnp.float32), 8, axis=0), TILE, axis=1)
-    edge = max(TILE, rows // 2)
+    edge = max(TILE, rows // 4)
     na = rows // edge
     own = jnp.stack(
         [own[:, a * edge : (a + 1) * edge, b * edge : (b + 1) * edge] for a in range(na) for b in range(2 * na)]

time: 501 us -> 692 us (1.38)
  Pallas kernels: 488 us -> 679 us
    pallas_call x1, Pallas kernels: 438 us -> 629 us  [gather_panels(): pl.pallas_call(functools.partial(gather_kernel, (layers, int_count, rows,...]
where the time goes in v5:
time: 692 us; the launch traced here: 688 us
  Pallas kernels  679 us (98%)
  local copies, waits for them, and re-layouts  8.05 us (1%)
    pallas_call x1, Pallas kernels, gather_panels(): pl.pallas_call(functools.partial(gather_kernel, (layers, int_count, rows,...  629 us
    pallas_call x1, Pallas kernels, predict(): pl.pallas_call(predict_kernel, grid_spec=pltpu.PrefetchScalarGridSpec(num...  50 us

profile of v5, /device:TPU:29, one launch (start us, length us, event | category | flops | bytes accessed | tf_op | source)
XLA Modules:
  0.0 688.4 jit_solution(7113411510662987858)
XLA Ops:
  0.0 2.5 dynamic-slice_bitcast_fusion
  2.5 0.0 copy-start.2
  3.0 0.0 copy-start.3
  3.0 0.0 copy-start.4
  3.4 0.0 copy-start
  3.4 2.0 copy-done
  5.4 0.0 copy-done.2
  5.4 0.1 fusion.32
  5.5 0.1 broadcast_in_dim.12
  5.6 0.0 copy-start.1
  5.7 2.2 copy-done.1
  7.8 629.3 %shard_map.46 = (f32[8,32,2,128,128]{4,3,2,1,0:T(8,128)}, f32[4,32,2,128,128]{4,3,2,1,0:T(8,128)}) custom-call(f32[32,2,128,128]{3,2,1,0:T(8,128)S(1)} %copy-done.1, f32[32,1024]{1,0:T(8,128)S(1)} %bitcast.142), custom_call_target="tpu_custom_call" | custom-call | tf_op jit(solution)/shard_map/pallas_call | solution.py:374
  637.2 0.0 copy-done.3
  637.2 0.6 convert_reduce_fusion.chosen
  637.8 0.0 copy-done.4
  637.8 0.6 copy.7.wavelet
  638.4 50.0 %shard_map.47 = f32[2,512,1024]{2,1,0:T(8,128)} custom-call(s32[1]{0:T(128)} %bitcast.my_block, f32[4,4,8,2,128,128]{5,4,3,2,1,0:T(8,128)} %bitcast.145, f32[8,4,8,2,128,128]{5,4,3,2,1,0:T(8,128)} %bitcast.143, f32[4,32]{1,0:T(4,128)} %convert_reduce_fusion.chosen, f32[8,4,8,2,128,128]{5,4,3,2,1,0:T(8,128)} %bitcast.144, f32[2,1]{1,0:T(2,128)} %copy.7.wavelet), custom_call_target="tpu_custom_call" | custom-call | tf_op jit(solution)/shard_map/pallas_call | solution.py:82
  (34 shorter events, 0.7 us)
Async XLA Ops:
  2.5 2.9 copy-start.2
  3.0 634.2 %copy-start.3 = (s32[4,24]{1,0:T(4,128)S(1)}, s32[4,24]{1,0:T(4,128)}, u32[]{:S(2)}) copy-start(s32[4,24]{1,0:T(4,128)} %param.6) | copy-start | bytes 1156
  3.0 634.8 %copy-start.4 = (f32[2,1]{0,1:T(1,128)S(1)}, f32[2,1]{0,1:T(1,128)}, u32[]{:S(2)}) copy-start(f32[2,1]{0,1:T(1,128)} %param.7) | copy-start | bytes 28
  3.4 2.0 copy-start
  5.6 2.2 copy-start.1

commit v6 on v4

--- a/solution.py
+++ b/solution.py
@@ -128,7 +128,9 @@
     def in_right(layer, core, a, b):
         return right.at[2 * layer + core, a * nb + b]
 
-    DOWN, UP, SIDE, ROW, TURN, RELAY = range(6)
+    DOWN, UP, SIDE, ROW, TURN, RELAY, FAR = range(7)
+    last = layers - 1
+    assert last > 1
 
     def remote(source, target, kind, j, r, where, sem=None):
         return pltpu.make_async_remote_copy(
@@ -146,6 +148,11 @@
         source = in_right(j, c, a, b) if source is None else source.at[a * nb + b]
         return remote(source, in_right(j, c, a, b), kind, j, r, device(*where, q))
 
+    def far_move(to, kind, r):
+        a, b = place(z, q, r)
+        target = in_right(z, c, a, b)
+        return remote(kept.at[a * nb + b], target, FAR, z, r, device(to, c, q), recv.at[kind, z, r])
+
     def arrival(kind, j, core, r):
         a, b = place(j, q, r)
         ref = in_right(j, core, a, b)
@@ -223,8 +230,15 @@
     def _():
         greet(z + 1, c, q)
 
-    ends = jnp.where(z > 0, 1, 0) + jnp.where(z < layers - 1, 1, 0)
-    pl.semaphore_wait(barrier, 2 * layers - 1 + ends)
+    @pl.when(z == 0)
+    def _():
+        greet(last, c, q)
+
+    @pl.when(z == last)
+    def _():
+        greet(0, c, q)
+
+    pl.semaphore_wait(barrier, 2 * layers + 1)
 
     def own_moves(r, do):
         @pl.when(z > 0)
@@ -234,6 +248,14 @@
         @pl.when(z < layers - 1)
         def _():
             do(move(UP, z, r, kept))
+
+        @pl.when(z == 0)
+        def _():
+            do(far_move(last, UP, r))
+
+        @pl.when(z == last)
+        def _():
+            do(far_move(0, DOWN, r))
 
         do(move(SIDE, z, r, kept))
         for other in range(layers):
@@ -276,7 +298,7 @@
             if waiting:
                 arrival(DOWN, j, c, r).wait_recv()
 
-            @pl.when(z > 0)
+            @pl.when((z > 1) | ((z > 0) & (j < last)))
             def _():
                 do(move(DOWN, j, r, None))
 
@@ -289,7 +311,7 @@
             if waiting:
                 arrival(UP, j, c, r).wait_recv()
 
-            @pl.when(z < layers - 1)
+            @pl.when((z < last - 1) | ((z < last) & (j > 0)))
             def _():
                 do(move(UP, j, r, None))
 
@@ -384,7 +406,7 @@
             pltpu.VMEM(own.shape, jnp.float32),
             pltpu.SemaphoreType.DMA((4, layers, rounds)),
             pltpu.SemaphoreType.DMA((rounds,)),
-            pltpu.SemaphoreType.DMA((6, layers, rounds)),
+            pltpu.SemaphoreType.DMA((7, layers, rounds)),
             pltpu.SemaphoreType.DMA((2, rounds)),
         ],
         compiler_params=pltpu.CompilerParams(

time: 501 us -> 635 us (1.27)
  the two profiles are of different devices: /device:TPU:29 before, /device:TPU:24 now
where the time goes in v6:
time: 635 us
  Pallas kernels  626 us (99%)
  local copies, waits for them, and re-layouts  7.73 us (1%)
    pallas_call x1, Pallas kernels, gather_panels(): pl.pallas_call(functools.partial(gather_kernel, (layers, int_count, rows,...  576 us
    pallas_call x1, Pallas kernels, predict(): pl.pallas_call(predict_kernel, grid_spec=pltpu.PrefetchScalarGridSpec(num...  49.9 us

profile of v6, /device:TPU:24, one launch (start us, length us, event | category | flops | bytes accessed | tf_op | source)
XLA Modules:
  0.0 635.0 jit_solution(6153023703818093810)
XLA Ops:
  0.0 2.5 dynamic-slice_bitcast_fusion
  2.5 0.0 copy-start.2
  2.7 0.0 copy-start.3
  2.7 0.0 copy-start.4
  2.9 0.0 copy-start
  2.9 2.0 copy-done
  4.9 0.0 copy-done.2
  4.9 0.1 fusion.8
  5.0 0.1 broadcast_in_dim.12
  5.1 0.0 copy-start.1
  5.1 2.2 copy-done.1
  7.3 576.4 %shard_map.46 = (f32[8,8,2,256,256]{4,3,2,1,0:T(8,128)}, f32[4,8,2,256,256]{4,3,2,1,0:T(8,128)}) custom-call(f32[8,2,256,256]{3,2,1,0:T(8,128)S(1)} %copy-done.1, f32[32,1024]{1,0:T(8,128)S(1)} %bitcast.46), custom_call_target="tpu_custom_call" | custom-call | tf_op jit(solution)/shard_map/pallas_call | solution.py:396
  583.8 0.0 copy-done.3
  583.8 0.6 convert_reduce_fusion.chosen
  584.4 0.0 copy-done.4
  584.4 0.6 copy.7.wavelet
  585.0 49.9 %shard_map.47 = f32[2,512,1024]{2,1,0:T(8,128)} custom-call(s32[1]{0:T(128)} %bitcast.my_block, f32[4,2,4,2,256,256]{5,4,3,2,1,0:T(8,128)} %bitcast.49, f32[8,2,4,2,256,256]{5,4,3,2,1,0:T(8,128)} %bitcast.47, f32[4,32]{1,0:T(4,128)} %convert_reduce_fusion.chosen, f32[8,2,4,2,256,256]{5,4,3,2,1,0:T(8,128)} %bitcast.48, f32[2,1]{1,0:T(2,128)} %copy.7.wavelet), custom_call_target="tpu_custom_call" | custom-call | tf_op jit(solution)/shard_map/pallas_call | solution.py:82
  (10 shorter events, 0.3 us)
Async XLA Ops:
  2.5 2.4 copy-start.2
  2.7 581.0 %copy-start.3 = (s32[4,24]{1,0:T(4,128)S(1)}, s32[4,24]{1,0:T(4,128)}, u32[]{:S(2)}) copy-start(s32[4,24]{1,0:T(4,128)} %param.6) | copy-start | bytes 1156
  2.7 581.7 %copy-start.4 = (f32[2,1]{0,1:T(1,128)S(1)}, f32[2,1]{0,1:T(1,128)}, u32[]{:S(2)}) copy-start(f32[2,1]{0,1:T(1,128)} %param.7) | copy-start | bytes 28
  2.9 2.0 copy-start
  5.1 2.2 copy-start.1
